TPU v7x, 32 devices: a whole 2x2x4 slice. The times are simulated.
32 devices in a mesh: clip: 4 (over z), row: 4 (over y, core), ch: 2 (over x).
Axes of the slice: x: 2, y: 2, z: 4, core: 2. Of those that a mesh axis runs over, the one named last changes fastest.
Arguments:
- features: bfloat16 [4, 4, 32, 512, 256], P('clip', None, 'row', None, 'ch'), may hold values from -6 to 6
- weight: bfloat16 [3, 3, 3, 3, 256], P(None, None, None, None, 'ch'), may hold values from -0.078125 to 0.078125
- target: bfloat16 [4, 3, 2, 32, 512], P('clip', None, None, 'row'), may hold values from -6 to 6
Outputs:
- grad_features: bfloat16 [4, 4, 32, 512, 256], P('clip', None, 'row', None, 'ch')
- grad_weight: float32 [3, 3, 3, 3, 256], P(None, None, None, None, 'ch')
- focal_loss: float32 [4], P('clip')
All inputs are finite; a program needn't handle non-finite values.
Results may differ from a plain program's by a relative error of at most 0.0049.
Values may be sent and summed in bfloat16 or wider, within the bound.
A program may use at most 64 MiB of HBM per device.

v0:
```python
import math

import jax
import jax.numpy as jnp
from jax import lax
from jax.sharding import PartitionSpec as P


def extended(x, sides, width):
    for axis, dim in sides:
        count, length = (lax.axis_size(axis), x.shape[dim])
        up = [(i, (i + 1) % count) for i in range(count - 1)]
        down = [(j, i) for i, j in up]
        last = lax.slice_in_dim(x, length - width, length, axis=dim)
        first = lax.slice_in_dim(x, 0, width, axis=dim)
        before = lax.ppermute(last, axis, up)
        after = lax.ppermute(first, axis, down)
        x = jnp.concatenate([before, x, after], axis=dim)
    return x


def column_table(columns):
    column_ids = jnp.arange(columns, dtype=jnp.int32)
    frequency_ids = jnp.arange(columns // 2, dtype=jnp.int32)
    phases = (
        2.0
        * math.pi
        / columns
        * (column_ids[:, None] * frequency_ids[None, :] % columns).astype(jnp.float32)
    )
    factor = 1.0 / math.sqrt(columns)
    return factor * jnp.stack([jnp.cos(phases), -jnp.sin(phases)], axis=1)


def row_table(height):
    row_ids = jnp.arange(height, dtype=jnp.int32)
    phases = (
        2.0 * math.pi / height * (row_ids[:, None] * row_ids[None, :] % height).astype(jnp.float32)
    )
    factor = 1.0 / math.sqrt(height)
    cosine = factor * jnp.cos(phases)
    sine_part = factor * jnp.sin(phases)
    return jnp.stack(
        [jnp.stack([cosine, -sine_part], axis=1), jnp.stack([sine_part, cosine], axis=1)], axis=0
    )


def tap_total(padded, frames_out, first_row, count, row_taps, columns):
    running = 0.0
    for time_tap in range(3):
        for row_tap in row_taps:
            for column_tap in range(3):
                begin = first_row + row_tap
                running = (
                    running
                    + padded[
                        :,
                        time_tap,
                        row_tap,
                        column_tap,
                        :,
                        time_tap : time_tap + frames_out,
                        begin : begin + count,
                        column_tap : column_tap + columns,
                    ]
                )
    return running


def shards(features, weight, target):
    clip_count, frames_in, rows_dev, columns, local_channels = features.shape
    frames_out = frames_in - 2
    kernel = weight.reshape(81, local_channels)
    tap_terms = jnp.einsum("kc,bfrwc->bkfrw", kernel, features, preferred_element_type=jnp.float32)
    tap_terms = tap_terms.reshape(clip_count, 3, 3, 3, 3, frames_in, rows_dev, columns)
    tap_terms = jnp.pad(tap_terms, ((0, 0),) * 6 + ((1, 1), (1, 1)))
    partial_out = tap_total(tap_terms, frames_out, 0, rows_dev, (0, 1, 2), columns)
    to_above = tap_total(tap_terms, frames_out, -1, 1, (2,), columns)
    to_below = tap_total(tap_terms, frames_out, rows_dev, 1, (0,), columns)
    rim_sums = extended(jnp.concatenate([to_above, to_below], axis=3), (("row", 3),), 1)
    from_above = jnp.pad(
        rim_sums[:, :, :, 0:1], ((0, 0), (0, 0), (0, 0), (0, rows_dev - 1), (0, 0))
    )
    from_below = jnp.pad(
        rim_sums[:, :, :, 3:4], ((0, 0), (0, 0), (0, 0), (rows_dev - 1, 0), (0, 0))
    )
    partial_out = partial_out + from_above + from_below
    summed = lax.psum(partial_out, "ch")
    height = rows_dev * lax.axis_size("row")
    entry_count = float(frames_out * 3 * height * (columns // 2))
    column_basis = column_table(columns)
    row_basis = row_table(height)
    residual = summed - target.astype(jnp.float32)
    spectra = jnp.einsum(
        "bofrw,wpk->bofpkr", residual, column_basis, precision=lax.Precision.HIGHEST
    )
    spectrum = jnp.einsum(
        "bofpkh,phqg->bofqkg",
        lax.all_to_all(spectra, "row", split_axis=4, concat_axis=5, tiled=True),
        row_basis,
        precision=lax.Precision.HIGHEST,
    )
    spectral_power = spectrum[:, :, :, 0] ** 2 + spectrum[:, :, :, 1] ** 2
    power_peak = lax.pmax(jnp.max(spectral_power, axis=(3, 4)), "row")
    focal_weight = spectral_power / (power_peak[:, :, :, None, None] + 1e-05)
    loss_part = jnp.sum(focal_weight * spectral_power, axis=(2, 3, 4)) / entry_count
    upstream = 2.0 * focal_weight[:, :, :, None] * spectrum
    row_grads = jnp.einsum(
        "bofqkg,phqg->bofpkh", upstream, row_basis, precision=lax.Precision.HIGHEST
    )
    column_grads = jnp.einsum(
        "bofpkr,wpk->bofrw",
        lax.all_to_all(row_grads, "row", split_axis=5, concat_axis=4, tiled=True),
        column_basis,
        precision=lax.Precision.HIGHEST,
    )
    loss_local = jnp.sum(loss_part, axis=1)
    grad_rounded = column_grads.astype(jnp.bfloat16)
    focal_loss = lax.psum(loss_local, "row")
    rimmed = extended(grad_rounded, (("row", 3),), 1)
    padded = jnp.pad(rimmed, ((0, 0), (0, 0), (2, 2), (0, 0), (1, 1)))
    tap_list = []
    for time_tap in range(3):
        for row_tap in range(3):
            for column_tap in range(3):
                tap_list.append(
                    padded[
                        :,
                        :,
                        2 - time_tap : 2 - time_tap + frames_in,
                        2 - row_tap : 2 - row_tap + rows_dev,
                        2 - column_tap : 2 - column_tap + columns,
                    ]
                )
    shifted = jnp.stack(tap_list, axis=1).reshape(clip_count, 81, frames_in, rows_dev, columns)
    gradient_in = jnp.einsum(
        "bkfrw,kc->bfrwc", shifted, kernel, preferred_element_type=jnp.float32
    ).astype(jnp.bfloat16)
    weight_part = jnp.einsum(
        "bkfrw,bfrwc->kc", shifted, features, preferred_element_type=jnp.float32
    )
    grad_weight = lax.psum(weight_part, ("clip", "row")).reshape(3, 3, 3, 3, local_channels)
    return (gradient_in, grad_weight, focal_loss)


def solution(mesh):
    placed = (
        P("clip", None, "row", None, "ch"),
        P(None, None, None, None, "ch"),
        P("clip", None, None, "row", None),
    )
    return jax.shard_map(
        shards,
        mesh=mesh,
        in_specs=placed,
        out_specs=(P("clip", None, "row", None, "ch"), P(None, None, None, None, "ch"), P("clip")),
        check_vma=False,
    )
```

profile of v0, /device:TPU:0, one launch (start us, length us, event | category | flops | bytes accessed | tf_op | source)
XLA Modules:
  0.0 175.7 jit_solution(607773618808863428)
XLA Ops:
  8.0 4.8 %fusion.6 = f32[1,81,4,8,512]{4,1,3,2,0:T(8,128)S(1)} fusion(bf16[1,4,8,512,128]{4,3,2,1,0:T(8,128)(2,1)} %param.3, bf16[81,128,1,1]{1,0,2,3:T(8,128)(2,1)S(1)} %reshape.840), kind=kOutput, calls=%fused_computation.43 | convolution fusion | flops 339738624 | bytes 9523456 | tf_op jit(solution)/shard_map/kc,bfrwc->bkfrw/dot_general | solution.py:74
  12.8 3.1 %copy.36 = f32[1,81,4,8,512]{4,3,2,1,0:T(8,128)S(1)} copy(f32[1,81,4,8,512]{4,1,3,2,0:T(8,128)S(1)} %fusion.6) | data formatting | bytes 10616832 | tf_op jit(solution)/shard_map/kc,bfrwc->bkfrw/transpose | solution.py:74
  16.3 2.4 %collective-permute-start = (f32[1,3,2,1,512]{4,3,2,1,0:T(1,128)S(1)}, f32[1,3,2,1,512]{4,3,2,1,0:T(1,128)S(1)}, u32[]{:S(2)}, u32[]{:S(2)}) collective-permute-start(f32[1,3,2,1,512]{4,3,2,1,0:T(1,128)S(1)} %get-tuple-element.3), channel_id=1, source_target_pairs={{0,2},{2,4},{4,6},{1,3},{3,5},{5,7},{8,10},{10,12},{12,14},{9,11},... | collective-permute-start | bytes 36872 | tf_op jit(solution)/shard_map/ppermute | solution.py:16
  18.6 1.3 collective-permute-start.1
  19.9 2.1 %sine_negate_fusion = (f32[512,1,256]{2,0,1:T(8,128)S(1)}, f32[512,1,256]{2,0,1:T(8,128)S(1)}) fusion(), kind=kLoop, calls=%fused_computation.69 | loop fusion | flops 1966080 | bytes 1048576 | tf_op jit(solution)/shard_map/neg | solution.py:32
  22.1 1.7 collective-permute-done.1
  23.9 1.2 pad_add_fusion
  25.2 24.0 %all-reduce.6.cloned.1.call-done = f32[1,3,2,8,512]{4,3,2,1,0:T(8,128)} async-done(((f32[1,3,2,8,512]{4,3,2,1,0:T(8,128)}), f32[1,3,2,8,512]{4,3,2,1,0:T(8,128)}) %all-reduce.6.cloned.1.call-update) | async-done | bytes 98320 | tf_op jit(solution)/shard_map/psum | solution.py:88
  49.2 1.7 convolution_bitcast_fusion.3
  51.9 3.1 %reshape.852 = f32[4,1,6144]{2,1,0:T(1,128)} reshape(f32[256,1,2,3,2,8]{5,4,3,2,1,0:T(2,128)S(1)} %bitcast.327) | data formatting | bytes 196608
  55.0 3.5 %all-to-all-start = ((f32[4,1,6144]{2,1,0:T(1,128)}), f32[4,1,6144]{2,1,0:T(1,128)S(1)}, u32[]{:S(2)}, u32[]{:S(2)}) async-start(f32[4,1,6144]{2,1,0:T(1,128)} %reshape.852), calls=%async_computation | async-start | bytes 196608 | tf_op jit(solution)/shard_map/all_to_all | solution.py:99
  58.5 4.1 %all-to-all-done = f32[4,1,6144]{2,1,0:T(1,128)S(1)} async-done(((f32[4,1,6144]{2,1,0:T(1,128)}), f32[4,1,6144]{2,1,0:T(1,128)S(1)}, u32[]{:S(2)}, u32[]{:S(2)}) %all-to-all-start) | async-done | bytes 98336 | tf_op jit(solution)/shard_map/all_to_all | solution.py:99
  64.0 2.4 %reshape.853 = f32[256,1,2,3,2,8]{5,4,3,2,1,0:T(2,128)S(1)} reshape(f32[4,6144]{1,0:T(4,128)S(1)} %reduce.5) | data formatting | bytes 196608
  66.4 1.1 copy.38
  68.1 5.7 %pmax.7 = f32[1,3,2]{1,2,0:T(2,128)S(1)} all-reduce(f32[1,3,2]{1,2,0:T(2,128)S(1)} %bitcast.332), channel_id=1, replica_groups=mesh['clip'=4,'row'=4,'ch'=2] {'row'}, use_global_device_ids=true, to_apply=%region_2.3 | all-reduce | flops 6 | bytes 48 | tf_op jit(solution)/shard_map/pmax | solution.py:104
  75.4 3.3 %all-to-all-start.1 = ((f32[4,1,6144]{2,1,0:T(1,128)}), f32[4,1,6144]{2,1,0:T(1,128)S(1)}, u32[]{:S(2)}, u32[]{:S(2)}) async-start(f32[4,1,6144]{2,1,0:T(1,128)} %reshape.854), calls=%async_computation.1 | async-start | bytes 196608 | tf_op jit(solution)/shard_map/all_to_all | solution.py:113
  78.9 4.1 %all-to-all-done.1 = f32[4,1,6144]{2,1,0:T(1,128)S(1)} async-done(((f32[4,1,6144]{2,1,0:T(1,128)}), f32[4,1,6144]{2,1,0:T(1,128)S(1)}, u32[]{:S(2)}, u32[]{:S(2)}) %all-to-all-start.1) | async-done | bytes 98336 | tf_op jit(solution)/shard_map/all_to_all | solution.py:113
  84.4 1.0 fusion.10
  85.4 1.5 collective-permute-start.2
  86.9 1.3 collective-permute-start.3
  88.8 7.8 %psum.23 = f32[1]{0:T(128)} all-reduce(f32[1]{0:T(128)} %bitcast.86), channel_id=1, replica_groups=mesh['clip'=4,'row'=4,'ch'=2] {'row'}, use_global_device_ids=true, to_apply=%region_6.7 | all-reduce | flops 1 | bytes 8 | tf_op jit(solution)/shard_map/psum | solution.py:119
  99.1 4.3 %convert_bitcast_fusion = bf16[1,4,8,512,128]{4,3,2,1,0:T(8,128)(2,1)} fusion(bf16[81,4,8,512]{3,2,1,0:T(8,128)(2,1)S(1)} %bitcast.325, bf16[81,128,1,1]{1,0,2,3:T(8,128)(2,1)S(1)} %reshape.840), kind=kOutput, calls=%fused_computation.40 | convolution fusion | flops 341835776 | bytes 6869248 | tf_op jit(solution)/shard_map/bkfrw,kc->bfrwc/dot_general | solution.py:136
  103.4 3.4 %fusion.11 = f32[81,128]{1,0:T(8,128)S(1)} fusion(bf16[1,4,8,512,128]{4,3,2,1,0:T(8,128)(2,1)S(1)} %copy-done, bf16[81,4,8,512]{3,2,1,0:T(8,128)(2,1)S(1)} %bitcast.326), kind=kOutput, calls=%fused_computation.50 | convolution fusion | flops 339738624 | bytes 6889984 | tf_op jit(solution)/shard_map/bkfrw,bfrwc->kc/dot_general | solution.py:139
  106.8 62.1 %psum.22 = f32[3,3,3,3,128]{4,3,2,1,0:T(4,128)} all-reduce(f32[3,3,3,3,128]{4,3,2,1,0:T(4,128)S(1)} %reshape.819), channel_id=1, replica_groups=mesh['clip'=4,'row'=4,'ch'=2] {'clip','row'}, use_global_device_ids=true, to_apply=%region_3.4 | all-reduce | flops 10368 | bytes 82944 | tf_op jit(solution)/shard_map/psum | solution.py:142
  (62 shorter events, 10.5 us)
Async XLA Ops:
  7.2 42.0 %all-reduce.6.cloned.1.call-start = ((), (), s32[]{:S(2)}) async-start(), calls=%async_computation.2 | async-start | bytes 196608 | tf_op jit(solution)/shard_map/psum | solution.py:88
  16.3 5.8 %collective-permute-start = (f32[1,3,2,1,512]{4,3,2,1,0:T(1,128)S(1)}, f32[1,3,2,1,512]{4,3,2,1,0:T(1,128)S(1)}, u32[]{:S(2)}, u32[]{:S(2)}) collective-permute-start(f32[1,3,2,1,512]{4,3,2,1,0:T(1,128)S(1)} %get-tuple-element.3), channel_id=1, source_target_pairs={{0,2},{2,4},{4,6},{1,3},{3,5},{5,7},{8,10},{10,12},{12,14},{9,11},... | collective-permute-start | bytes 36872 | tf_op jit(solution)/shard_map/ppermute | solution.py:16
  18.6 5.2 %collective-permute-start.1 = (f32[1,3,2,1,512]{4,3,2,1,0:T(1,128)S(1)}, f32[1,3,2,1,512]{4,3,2,1,0:T(1,128)S(1)}, u32[]{:S(2)}, u32[]{:S(2)}) collective-permute-start(f32[1,3,2,1,512]{4,3,2,1,0:T(1,128)S(1)} %get-tuple-element.4), channel_id=1, source_target_pairs={{2,0},{4,2},{6,4},{3,1},{5,3},{7,5},{10,8},{12,10},{14,12},{11,9},... | collective-permute-start | bytes 36872 | tf_op jit(solution)/shard_map/ppermute | solution.py:17
  22.1 27.0 %copy-start.1 = (bf16[1,3,2,8,512]{4,3,2,1,0:T(8,128)(2,1)S(1)}, bf16[1,3,2,8,512]{4,3,2,1,0:T(8,128)(2,1)}, u32[]{:S(2)}) copy-start(bf16[1,3,2,8,512]{4,3,2,1,0:T(8,128)(2,1)} %param.5) | copy-start | bytes 147460
  55.0 7.6 %all-to-all-start = ((f32[4,1,6144]{2,1,0:T(1,128)}), f32[4,1,6144]{2,1,0:T(1,128)S(1)}, u32[]{:S(2)}, u32[]{:S(2)}) async-start(f32[4,1,6144]{2,1,0:T(1,128)} %reshape.852), calls=%async_computation | async-start | bytes 196608 | tf_op jit(solution)/shard_map/all_to_all | solution.py:99
  75.4 7.6 %all-to-all-start.1 = ((f32[4,1,6144]{2,1,0:T(1,128)}), f32[4,1,6144]{2,1,0:T(1,128)S(1)}, u32[]{:S(2)}, u32[]{:S(2)}) async-start(f32[4,1,6144]{2,1,0:T(1,128)} %reshape.854), calls=%async_computation.1 | async-start | bytes 196608 | tf_op jit(solution)/shard_map/all_to_all | solution.py:113
  85.4 11.2 %collective-permute-start.2 = (bf16[1,3,2,1,512]{4,3,2,1,0:T(2,128)(2,1)S(1)}, bf16[1,3,2,1,512]{4,3,2,1,0:T(2,128)(2,1)S(1)}, u32[]{:S(2)}, u32[]{:S(2)}) collective-permute-start(bf16[1,3,2,1,512]{4,3,2,1,0:T(2,128)(2,1)S(1)} %get-tuple-element.5), channel_id=1, source_target_pairs={{0,2},{2,4},{4,6},{1,3},{3,5},{5,7},{8,10},{10,12},{12,14},{9,11},... | collective-permute-start | bytes 18440 | tf_op jit(solution)/shard_map/ppermute | solution.py:16
  86.9 9.7 %collective-permute-start.3 = (bf16[1,3,2,1,512]{4,3,2,1,0:T(2,128)(2,1)S(1)}, bf16[1,3,2,1,512]{4,3,2,1,0:T(2,128)(2,1)S(1)}, u32[]{:S(2)}, u32[]{:S(2)}) collective-permute-start(bf16[1,3,2,1,512]{4,3,2,1,0:T(2,128)(2,1)S(1)} %get-tuple-element.6), channel_id=1, source_target_pairs={{2,0},{4,2},{6,4},{3,1},{5,3},{7,5},{10,8},{12,10},{14,12},{11,9},... | collective-permute-start | bytes 18440 | tf_op jit(solution)/shard_map/ppermute | solution.py:17
  99.1 4.3 %copy-start = (bf16[1,4,8,512,128]{4,3,2,1,0:T(8,128)(2,1)S(1)}, bf16[1,4,8,512,128]{4,3,2,1,0:T(8,128)(2,1)}, u32[]{:S(2)}) copy-start(bf16[1,4,8,512,128]{4,3,2,1,0:T(8,128)(2,1)} %param.3) | copy-start | bytes 12582916
Sparse Core Ops, SparseCore 0:
  25.2 23.9 all-reduce.5
where the time goes:
time: 176 us
  blocking collectives  75.6 us (43%)
  waiting for transfers between devices  33.9 us (19%)
  matrix products  16 us (9%)
  local copies, waits for them, and re-layouts  15.9 us (9%)
  between operations  14.4 us (8%)
  starting transfers between devices  13.2 us (8%)
  other arithmetic  6.74 us (4%)
    psum x1, blocking collectives, shards(): lax.psum(weight_part, ('clip', 'row')).reshape(3, 3, 3, 3, local_channels)  62.1 us
    psum x1, waiting for transfers between devices, shards(): summed = lax.psum(partial_out, 'ch')  24 us
    unnamed x34, local copies, waits for them, and re-layouts  8.75 us
    psum x1, blocking collectives, shards(): focal_loss = lax.psum(loss_local, 'row')  7.79 us
    pmax x1, blocking collectives, shards(): power_peak = lax.pmax(jnp.max(spectral_power, axis=(3, 4)), 'row')  5.73 us
    dot_general x1, matrix products, shards(): jnp.einsum('kc,bfrwc->bkfrw', kernel, features, preferred_element_type=jn...  4.83 us
    dot_general x1, matrix products, shards(): jnp.einsum('bkfrw,kc->bfrwc', shifted, kernel, preferred_element_type=jnp...  4.34 us
    all_to_all x1, waiting for transfers between devices, shards(): lax.all_to_all(row_grads, 'row', split_axis=5, concat_axis=4, tiled=True)  4.08 us
  transfers between devices with their start and end apart: 7, of which 4 were waited for; matrix products, arithmetic and copies ran while one was open for 2% of the time, Pallas kernels for 0%

commit v1 on v0

v1 whole, which is shorter than its diff:
```python
import functools
import math

import jax
import jax.numpy as jnp
import ml_dtypes
import numpy as np
from jax import lax
from jax.experimental import pallas as pl
from jax.experimental.pallas import tpu as pltpu
from jax.sharding import PartitionSpec as P

MESH = pl.DeviceIdType.MESH
BLOCK = 16
F32 = jnp.float32
BF16 = jnp.bfloat16


def split_table(table):
    high = table.astype(ml_dtypes.bfloat16)
    low = (table - high.astype(np.float64)).astype(ml_dtypes.bfloat16)
    return high, low


def column_table(columns):
    phases = np.outer(np.arange(columns), np.arange(columns // 2)) % columns
    phases = 2.0 * math.pi / columns * phases
    return np.concatenate([np.cos(phases), -np.sin(phases)], axis=1) / math.sqrt(columns)


def row_table(height, rows_dev):
    table = np.zeros((2 * height, height // rows_dev * BLOCK))
    ids = np.arange(height)
    for device in range(height // rows_dev):
        for entry in range(rows_dev + 2):
            row = device * rows_dev + rows_dev - entry
            if 0 <= row < height:
                phase = 2.0 * math.pi / height * (ids * row % height)
                table[:height, device * BLOCK + entry] = np.cos(phase)
                table[height:, device * BLOCK + entry] = -np.sin(phase)
    return table / math.sqrt(height)


def halves(x):
    high = x.astype(BF16)
    return high, (x - high.astype(F32)).astype(BF16)


def dot(a, b, dims=((1,), (0,))):
    return lax.dot_general(a, b, (dims, ((), ())), preferred_element_type=F32)


def dot3(a, b, dims=((1,), (0,))):
    return dot(a[0], b[0], dims) + (dot(a[0], b[1], dims) + dot(a[1], b[0], dims))


def shift(x, by):
    columns = x.shape[-1]
    lane = lax.broadcasted_iota(jnp.int32, x.shape, 1)
    if by > 0:
        return jnp.where(lane < by, 0.0, pltpu.roll(x, by, 1))
    return jnp.where(lane >= columns + by, 0.0, pltpu.roll(x, columns + by, 1))


def main_kernel(
    sizes,
    features,
    weight,
    target,
    row_high,
    row_low,
    back_high,
    back_low,
    col_high_any,
    col_low_any,
    shifted_out,
    weight_out,
    grad_weight,
    loss_out,
    held,
    col_high,
    col_low,
    acc,
    weight_acc,
    part,
    arrived,
    grad_send,
    grad_all,
    shifted,
    kernel_acc,
    terms,
    terms_in,
    terms_sum,
    load_sem,
    send_sem,
    recv_sem,
    back_send,
    back_recv,
    terms_send,
    terms_recv,
    sum_send,
    sum_recv,
):
    n_clip, n_row, n_ch, chunk, n_own = sizes
    frames_in, rows_dev, columns, channels = held.shape
    frames_out = frames_in - 2
    planes = 3 * frames_out
    n_group = n_row * n_ch
    n_all = n_clip * n_row
    clip, row, ch = (lax.axis_index(a) for a in ("clip", "row", "ch"))
    me = row * n_ch + ch
    rank = clip * n_row + row
    entries = float(planes * n_row * rows_dev * (columns // 2))

    loads = [
        pltpu.make_async_copy(features.at[0, f], held.at[f], load_sem.at[f])
        for f in range(frames_in)
    ]
    loads.append(pltpu.make_async_copy(col_high_any, col_high, load_sem.at[frames_in]))
    loads.append(pltpu.make_async_copy(col_low_any, col_low, load_sem.at[frames_in + 1]))
    for load in loads:
        load.start()

    barrier = pltpu.get_barrier_semaphore()

    @pl.loop(1, n_group)
    def _(p):
        other = lax.rem(me + p, n_group)
        pl.semaphore_signal(
            barrier,
            inc=1,
            device_id={"row": other // n_ch, "ch": lax.rem(other, n_ch)},
            device_id_type=MESH,
        )

    @pl.loop(n_row, n_all)
    def _(p):
        other = lax.rem(clip * n_row + p, n_all)
        pl.semaphore_signal(
            barrier,
            inc=1,
            device_id={"clip": other // n_row, "row": lax.rem(other, n_row)},
            device_id_type=MESH,
        )

    weight_acc[...] = jnp.zeros_like(weight_acc)
    for dt in range(3):
        for di in range(3):
            for dj in range(3):
                at = (dt * 3 + di) * BLOCK + dj * 3
                weight_acc[at : at + 3, :] = weight[dt, di, dj].astype(F32)
    taps = weight_acc[...].astype(BF16)
    weight_out[...] = taps

    acc[...] = jnp.zeros_like(acc)

    @pl.when(ch == 0)
    def _():
        for t in range(frames_out):
            for o in range(3):
                frame = -target[0, o, t].astype(F32)
                for i in range(rows_dev):
                    acc[t, rows_dev - i, 3 + o, :] = frame[i]

    def exchange(t):
        for o in range(3):
            views = [acc[t, :, dj * 3 + o, :] for dj in range(3)]
            part[t * 3 + o] = views[1] + shift(views[0], 1) + shift(views[2], -1)
            plane = t * 3 + o

            @pl.when(me == plane)
            def _():
                arrived[plane] = part[plane]

            @pl.when(me != plane)
            def _():
                pltpu.make_async_remote_copy(
                    src_ref=part.at[plane],
                    dst_ref=arrived.at[me],
                    send_sem=send_sem.at[plane],
                    recv_sem=recv_sem.at[me],
                    device_id={"row": plane // n_ch, "ch": plane % n_ch},
                    device_id_type=MESH,
                ).start()

    for f in range(frames_in):
        loads[f].wait()
        low, top = max(0, f - frames_out + 1), min(2, f)
        chosen = taps[low * 3 * BLOCK : (top + 1) * 3 * BLOCK]

        @pl.loop(0, rows_dev, unroll=True)
        def _(r):
            made = dot(chosen, held[f, r], ((1,), (1,))).reshape(-1, BLOCK, columns)
            for dt in range(low, top + 1):
                at = (dt - low) * 3
                acc[f - dt, pl.ds(rows_dev - 1 - r, 3)] += made[at : at + 3]

        if f == 2:
            pl.semaphore_wait(barrier, n_group - 1 + n_all - n_row)
        if f >= 2:
            exchange(f - 2)

    loads[frames_in].wait()
    loads[frames_in + 1].wait()

    @pl.when(me < planes)
    def _():
        @pl.loop(0, n_group)
        def _(s):
            @pl.when(s != me)
            def _():
                pltpu.make_async_copy(
                    arrived.at[s], arrived.at[s], recv_sem.at[s]
                ).wait()

        blocks = []
        for r in range(n_row):
            total = arrived[r * n_ch]
            for c in range(1, n_ch):
                total = total + arrived[r * n_ch + c]
            blocks.append(total)
        residual = jnp.concatenate(blocks, axis=0)
        height = n_row * rows_dev
        half = columns // 2
        basis = (col_high[...], col_low[...])
        rows_done = dot3((row_high[...], row_low[...]), halves(residual))
        both = dot3(halves(rows_done), basis)
        real = both[:height, :half] - both[height:, half:]
        imag = both[height:, :half] + both[:height, half:]
        power = real * real + imag * imag
        peak = jnp.max(power, keepdims=True)
        focal = power / (peak + 1e-05)
        loss = jnp.sum(focal * power, keepdims=True) / entries
        up_real = 2.0 * focal * real
        up_imag = 2.0 * focal * imag
        upstream = jnp.concatenate(
            [
                jnp.concatenate([up_real, up_imag], axis=1),
                jnp.concatenate([up_imag, -up_real], axis=1),
            ],
            axis=0,
        )
        columns_done = dot3(halves(upstream), basis, ((1,), (1,)))
        grads = dot3((back_high[...], back_low[...]), halves(columns_done))
        loss_high = loss.astype(BF16).astype(F32)
        loss_mid = (loss - loss_high).astype(BF16).astype(F32)
        loss_low = loss - loss_high - loss_mid
        entry = lax.rem(lax.broadcasted_iota(jnp.int32, grads.shape, 0), BLOCK)
        grads = jnp.where(entry == rows_dev + 2, loss_high, grads)
        grads = jnp.where(entry == rows_dev + 3, loss_mid, grads)
        grads = jnp.where(entry == rows_dev + 4, loss_low, grads)
        grads = grads.astype(BF16)
        for r in range(n_row):
            grad_send[r] = grads[r * BLOCK : (r + 1) * BLOCK]

        @pl.loop(1, n_group)
        def _(p):
            other = lax.rem(me + p, n_group)
            pltpu.make_async_remote_copy(
                src_ref=grad_send.at[other // n_ch],
                dst_ref=grad_all.at[me],
                send_sem=back_send.at[p],
                recv_sem=back_recv.at[me],
                device_id={"row": other // n_ch, "ch": lax.rem(other, n_ch)},
                device_id_type=MESH,
            ).start()

        grad_all[me] = grad_send[row]

    acc[...] = jnp.zeros_like(acc)
    for plane in range(planes):
        @pl.when(me != plane)
        def _():
            pltpu.make_async_copy(
                grad_all.at[plane], grad_all.at[plane], back_recv.at[plane]
            ).wait()

    loss_total = jnp.zeros((1, 128), F32)
    for plane in range(planes):
        t, o = divmod(plane, 3)
        grads = grad_all[plane].astype(F32)
        for part_at in range(3):
            at = rows_dev + 2 + part_at
            loss_total = loss_total + grads[at : at + 1, :128]
        entry = lax.broadcasted_iota(jnp.int32, grads.shape, 0)
        grads = jnp.where(entry < rows_dev + 2, grads, 0.0)
        for dj in range(3):
            moved = grads if dj == 1 else shift(grads, dj - 1)
            acc[t, :, dj * 3 + o, :] = moved
    loss_out[...] = loss_total
    for t in range(frames_out):
        shifted[t] = acc[t].reshape(BLOCK * BLOCK, columns).astype(BF16)
    shifted_out[...] = shifted[...]

    kernel_acc[...] = jnp.zeros_like(kernel_acc)

    for f in range(frames_in):
        low, top = max(0, f - frames_out + 1), min(2, f)
        total = 0.0
        for r in range(rows_dev):
            begin = (rows_dev - 1 - r) * BLOCK
            stack = jnp.concatenate(
                [shifted[f - dt, begin : begin + 3 * BLOCK, :] for dt in range(low, top + 1)],
                axis=0,
            )
            total = total + dot(stack, held[f, r])
        kernel_acc[low * 3 * BLOCK : (top + 1) * 3 * BLOCK, :] += total

    terms[...] = jnp.zeros_like(terms)
    for b in range(9):
        terms[b * 9 : b * 9 + 9, :] = kernel_acc[b * BLOCK : b * BLOCK + 9, :]

    for m in range(n_own):
        @pl.when(rank == m)
        def _():
            terms_in[m] = terms[m * chunk : (m + 1) * chunk, :]

        @pl.when(rank != m)
        def _():
            pltpu.make_async_remote_copy(
                src_ref=terms.at[pl.ds(m * chunk, chunk)],
                dst_ref=terms_in.at[rank],
                send_sem=terms_send.at[m],
                recv_sem=terms_recv.at[rank],
                device_id={"clip": m // n_row, "row": m % n_row},
                device_id_type=MESH,
            ).start()

    @pl.when(rank < n_own)
    def _():
        @pl.loop(0, n_all)
        def _(s):
            @pl.when(s != rank)
            def _():
                pltpu.make_async_copy(
                    terms_in.at[s], terms_in.at[s], terms_recv.at[s]
                ).wait()

        terms_sum[rank] = jnp.sum(terms_in[...], axis=0)

        @pl.loop(1, n_all)
        def _(p):
            other = lax.rem(rank + p, n_all)
            pltpu.make_async_remote_copy(
                src_ref=terms_sum.at[rank],
                dst_ref=terms_sum.at[rank],
                send_sem=sum_send.at[p],
                recv_sem=sum_recv.at[rank],
                device_id={"clip": other // n_row, "row": lax.rem(other, n_row)},
                device_id_type=MESH,
            ).start()

    for m in range(n_own):
        @pl.when(rank != m)
        def _():
            pltpu.make_async_copy(
                terms_sum.at[m], terms_sum.at[m], sum_recv.at[m]
            ).wait()

    for k in range(27):
        dt, di, dj = k // 9, k // 3 % 3, k % 3
        for o in range(3):
            m, at = divmod(k * 3 + o, chunk)
            grad_weight[dt, di, dj, o : o + 1, :] = terms_sum[m, at : at + 1, :]

    for plane in range(planes):
        @pl.when(me != plane)
        def _():
            pltpu.make_async_copy(part.at[plane], part.at[plane], send_sem.at[plane]).wait()

    @pl.when(me < planes)
    def _():
        @pl.loop(1, n_group)
        def _(p):
            pltpu.make_async_copy(grad_send.at[0], grad_send.at[0], back_send.at[p]).wait()

    for m in range(n_own):
        @pl.when(rank != m)
        def _():
            piece = terms.at[pl.ds(m * chunk, chunk)]
            pltpu.make_async_copy(piece, piece, terms_send.at[m]).wait()

    @pl.when(rank < n_own)
    def _():
        @pl.loop(1, n_all)
        def _(p):
            pltpu.make_async_copy(
                terms_sum.at[rank], terms_sum.at[rank], sum_send.at[p]
            ).wait()


def features_kernel(frames_out, shifted, taps, grad):
    rows_dev, columns, channels = grad.shape[2:]
    for f in range(frames_out + 2):
        @pl.when(pl.program_id(0) == f)
        def _():
            low, top = max(0, f - frames_out + 1), min(2, f)
            chosen = taps[low * 3 * BLOCK : (top + 1) * 3 * BLOCK, :]
            for r in range(rows_dev):
                begin = (rows_dev - 1 - r) * BLOCK
                stack = jnp.concatenate(
                    [shifted[f - dt, begin : begin + 3 * BLOCK, :] for dt in range(low, top + 1)],
                    axis=0,
                )
                grad[0, 0, r] = dot(stack, chosen, ((0,), (0,))).astype(BF16)


def shards(features, weight, target):
    _, frames_in, rows_dev, columns, channels = features.shape
    frames_out = frames_in - 2
    planes = 3 * frames_out
    n_clip, n_row, n_ch = (lax.axis_size(a) for a in ("clip", "row", "ch"))
    n_group, n_all = n_row * n_ch, n_clip * n_row
    assert planes <= n_group and rows_dev + 5 <= BLOCK
    height = n_row * rows_dev
    pieces = -(-81 // 8)
    chunk = 8 * -(-pieces // n_all)
    n_own = -(-81 // chunk)
    rows = row_table(height, rows_dev)
    tables = (
        *split_table(rows),
        *split_table(np.ascontiguousarray(rows.T)),
        *split_table(column_table(columns)),
    )
    vmem = pl.BlockSpec(memory_space=pltpu.VMEM)
    anywhere = pl.BlockSpec(memory_space=pl.ANY)
    dma = pltpu.SemaphoreType.DMA
    shifted, taps, grad_weight, loss = pl.pallas_call(
        functools.partial(main_kernel, (n_clip, n_row, n_ch, chunk, n_own)),
        out_shape=(
            jax.ShapeDtypeStruct((frames_out, BLOCK * BLOCK, columns), BF16),
            jax.ShapeDtypeStruct((9 * BLOCK, channels), BF16),
            jax.ShapeDtypeStruct((3, 3, 3, 3, channels), F32),
            jax.ShapeDtypeStruct((1, 128), F32),
        ),
        in_specs=[anywhere] + [vmem] * 6 + [anywhere] * 2,
        out_specs=(vmem,) * 4,
        scratch_shapes=[
            pltpu.VMEM((frames_in, rows_dev, columns, channels), BF16),
            pltpu.VMEM((columns, columns), BF16),
            pltpu.VMEM((columns, columns), BF16),
            pltpu.VMEM((frames_out, BLOCK, BLOCK, columns), F32),
            pltpu.VMEM((9 * BLOCK, channels), F32),
            pltpu.VMEM((planes, BLOCK, columns), F32),
            pltpu.VMEM((n_group, BLOCK, columns), F32),
            pltpu.VMEM((n_row, BLOCK, columns), BF16),
            pltpu.VMEM((planes, BLOCK, columns), BF16),
            pltpu.VMEM((frames_out, BLOCK * BLOCK, columns), BF16),
            pltpu.VMEM((9 * BLOCK, channels), F32),
            pltpu.VMEM((n_own * chunk, channels), F32),
            pltpu.VMEM((n_all, chunk, channels), F32),
            pltpu.VMEM((n_own, chunk, channels), F32),
            dma((frames_in + 2,)),
            dma((planes,)),
            dma((n_group,)),
            dma((n_group,)),
            dma((planes,)),
            dma((n_own,)),
            dma((n_all,)),
            dma((n_all,)),
            dma((n_own,)),
        ],
        compiler_params=pltpu.CompilerParams(
            collective_id=0, has_side_effects=True, vmem_limit_bytes=48 * 1024 * 1024
        ),
        name="main",
    )(features, weight, target, *tables)
    grad_features = pl.pallas_call(
        functools.partial(features_kernel, frames_out),
        grid=(frames_in,),
        out_shape=jax.ShapeDtypeStruct(features.shape, BF16),
        in_specs=[
            pl.BlockSpec(shifted.shape, lambda f: (0, 0, 0)),
            pl.BlockSpec(taps.shape, lambda f: (0, 0)),
        ],
        out_specs=pl.BlockSpec(
            (1, 1, rows_dev, columns, channels), lambda f: (0, f, 0, 0, 0)
        ),
        compiler_params=pltpu.CompilerParams(vmem_limit_bytes=48 * 1024 * 1024),
        name="features",
    )(shifted, taps)
    return (grad_features, grad_weight, loss[0, :1])


def solution(mesh):
    placed = (
        P("clip", None, "row", None, "ch"),
        P(None, None, None, None, "ch"),
        P("clip", None, None, "row", None),
    )
    return jax.shard_map(
        shards,
        mesh=mesh,
        in_specs=placed,
        out_specs=(P("clip", None, "row", None, "ch"), P(None, None, None, None, "ch"), P("clip")),
        check_vma=False,
    )
```

time: 176 us -> 41.5 us (0.24)
  blocking collectives: 75.6 us -> 0 us
  waiting for transfers between devices: 33.9 us -> 0 us
  Pallas kernels: 0 us -> 29.8 us
  matrix products: 16 us -> 0 us
  starting transfers between devices: 13.2 us -> 0 us
  between operations: 14.4 us -> 1.82 us
  other arithmetic: 6.74 us -> 0 us
  local copies, waits for them, and re-layouts: 15.9 us -> 9.29 us
    psum x2 -> x0, blocking collectives: 69.9 us -> none  [the longest x1 62.1 us: shards(): lax.psum(weight_part, ('clip', 'row')).reshape(3, 3, 3, 3, local_channels)]
    pallas_call x0 -> x2, Pallas kernels: none -> 29.8 us  [the longest x1 26.3 us: shards(): pl.pallas_call(functools.partial(main_kernel, (n_clip, n_row, n_ch, chunk...]
    psum x1 -> x0, waiting for transfers between devices: 24 us -> none  [shards(): summed = lax.psum(partial_out, 'ch')]
    dot_general x7 -> x0, matrix products: 16 us -> none  [the longest x1 4.83 us: shards(): jnp.einsum('kc,bfrwc->bkfrw', kernel, features, preferred_element_type=jn...]
    all_to_all x2 -> x0, waiting for transfers between devices: 8.14 us -> none  [the longest x1 4.08 us: shards(): lax.all_to_all(row_grads, 'row', split_axis=5, concat_axis=4, tiled=True)]
    all_to_all x2 -> x0, starting transfers between devices: 6.79 us -> none  [the longest x1 3.49 us: shards(): lax.all_to_all(spectra, 'row', split_axis=4, concat_axis=5, tiled=True)]
    ppermute x4 -> x0, starting transfers between devices: 6.4 us -> none  [the longest x2 3.82 us: extended(): before = lax.ppermute(last, axis, up)]
    pmax x1 -> x0, blocking collectives: 5.73 us -> none  [shards(): power_peak = lax.pmax(jnp.max(spectral_power, axis=(3, 4)), 'row')]
  transfers between devices with their start and end apart: 7 -> 0, of which waited for: 4 -> 0; matrix products, arithmetic and copies ran while one was open for 2% -> 0% of each run, Pallas kernels for 0% -> 0%
where the time goes in v1:
time: 41.5 us; the launch traced here: 40.9 us
  Pallas kernels  29.8 us (72%)
  local copies, waits for them, and re-layouts  9.29 us (22%)
  between operations  1.82 us (4%)
    pallas_call x1, Pallas kernels, shards(): pl.pallas_call(functools.partial(main_kernel, (n_clip, n_row, n_ch, chunk...  26.3 us
    unnamed x19, local copies, waits for them, and re-layouts  9.29 us
    pallas_call x1, Pallas kernels, shards(): pl.pallas_call(functools.partial(features_kernel, frames_out), grid=(fram...  3.43 us

profile of v1, /device:TPU:0, one launch (start us, length us, event | category | flops | bytes accessed | tf_op | source)
XLA Modules:
  0.0 40.9 jit_solution(16962958112390961449)
XLA Ops:
  0.6 0.0 copy-start
  0.6 2.2 %copy-done = bf16[1,4,8,512,128]{4,3,2,1,0:T(8,128)(2,1)S(1)} copy-done((bf16[1,4,8,512,128]{4,3,2,1,0:T(8,128)(2,1)S(1)}, bf16[1,4,8,512,128]{4,3,2,1,0:T(8,128)(2,1)}, u32[]{:S(2)}) %copy-start) | copy-done | bytes 4194328
  2.8 0.0 copy-start.1
  2.8 1.0 %copy-done.1 = bf16[512,512]{1,0:T(8,128)(2,1)S(1)} copy-done((bf16[512,512]{1,0:T(8,128)(2,1)S(1)}, bf16[512,512]{1,0:T(8,128)(2,1)}, u32[]{:S(2)}) %copy-start.1) | copy-done | bytes 524312
  3.9 0.0 copy-start.2
  3.9 1.0 %copy-done.2 = bf16[512,512]{1,0:T(8,128)(2,1)S(1)} copy-done((bf16[512,512]{1,0:T(8,128)(2,1)S(1)}, bf16[512,512]{1,0:T(8,128)(2,1)}, u32[]{:S(2)}) %copy-start.2) | copy-done | bytes 524312
  4.9 0.0 copy-start.3
  4.9 0.8 %copy-done.3 = bf16[1,3,2,8,512]{4,3,2,1,0:T(8,128)(2,1)S(1)} copy-done((bf16[1,3,2,8,512]{4,3,2,1,0:T(8,128)(2,1)S(1)}, bf16[1,3,2,8,512]{4,3,2,1,0:T(8,128)(2,1)}, u32[]{:S(2)}) %copy-start.3) | copy-done | bytes 49176
  5.7 0.0 copy-start.4
  5.7 0.7 %copy-done.4 = bf16[3,3,3,3,128]{4,3,2,1,0:T(4,128)(2,1)S(1)} copy-done((bf16[3,3,3,3,128]{4,3,2,1,0:T(4,128)(2,1)S(1)}, bf16[3,3,3,3,128]{4,3,2,1,0:T(4,128)(2,1)}, u32[]{:S(2)}) %copy-start.4) | copy-done | bytes 20760
  6.4 0.0 copy-start.5
  6.5 0.7 %copy-done.5 = bf16[64,64]{1,0:T(8,128)(2,1)S(1)} copy-done((bf16[64,64]{1,0:T(8,128)(2,1)S(1)}, bf16[64,64]{1,0:T(8,128)(2,1)}, u32[]{:S(2)}) %copy-start.5) | copy-done | bytes 8216
  7.2 0.0 copy-start.6
  7.2 0.7 %copy-done.6 = bf16[64,64]{1,0:T(8,128)(2,1)S(1)} copy-done((bf16[64,64]{1,0:T(8,128)(2,1)S(1)}, bf16[64,64]{1,0:T(8,128)(2,1)}, u32[]{:S(2)}) %copy-start.6) | copy-done | bytes 8216
  7.9 0.0 copy-start.7
  7.9 0.7 %copy-done.7 = bf16[64,64]{1,0:T(8,128)(2,1)S(1)} copy-done((bf16[64,64]{1,0:T(8,128)(2,1)S(1)}, bf16[64,64]{1,0:T(8,128)(2,1)}, u32[]{:S(2)}) %copy-start.7) | copy-done | bytes 8216
  8.6 0.0 copy-start.8
  8.6 0.7 %copy-done.8 = bf16[64,64]{1,0:T(8,128)(2,1)S(1)} copy-done((bf16[64,64]{1,0:T(8,128)(2,1)S(1)}, bf16[64,64]{1,0:T(8,128)(2,1)}, u32[]{:S(2)}) %copy-start.8) | copy-done | bytes 8216
  9.3 26.3 %main.1 = (bf16[2,256,512]{2,1,0:T(8,128)(2,1)S(1)}, bf16[144,128]{1,0:T(8,128)(2,1)S(1)}, f32[3,3,3,3,128]{4,3,2,1,0:T(4,128)S(1)}, f32[1,128]{1,0:T(1,128)S(1)}) custom-call(bf16[1,4,8,512,128]{4,3,2,1,0:T(8,128)(2,1)S(1)} %copy-done, bf16[3,3,3,3,128]{4,3,2,1,0:T(4,128)(2,1)S(1)} %copy-done.4, bf16[1,3,2,8,512]{4,3,2,1,0:T(8,128)(2,1)S(1)} %copy-done.3, ...), custom_call_target="tpu_custom_call" | custom-call | tf_op jit(solution)/shard_map/main/pallas_call | solution.py:428
  35.7 3.4 %features.3 = bf16[1,4,8,512,128]{4,3,2,1,0:T(8,128)(2,1)} custom-call(bf16[2,256,512]{2,1,0:T(8,128)(2,1)S(1)} %get-tuple-element.7.shifted, bf16[144,128]{1,0:T(8,128)(2,1)S(1)} %get-tuple-element.8.taps), custom_call_target="tpu_custom_call" | custom-call | tf_op jit(solution)/shard_map/features/pallas_call | solution.py:468
  39.1 0.6 %copy.14 = f32[3,3,3,3,128]{4,3,2,1,0:T(4,128)} copy(f32[3,3,3,3,128]{4,3,2,1,0:T(4,128)S(1)} %get-tuple-element.15) | data formatting | bytes 82944
Async XLA Ops:
  0.6 2.2 %copy-start = (bf16[1,4,8,512,128]{4,3,2,1,0:T(8,128)(2,1)S(1)}, bf16[1,4,8,512,128]{4,3,2,1,0:T(8,128)(2,1)}, u32[]{:S(2)}) copy-start(bf16[1,4,8,512,128]{4,3,2,1,0:T(8,128)(2,1)} %features.2) | copy-start | bytes 12582916
  2.8 1.0 %copy-start.1 = (bf16[512,512]{1,0:T(8,128)(2,1)S(1)}, bf16[512,512]{1,0:T(8,128)(2,1)}, u32[]{:S(2)}) copy-start(bf16[512,512]{1,0:T(8,128)(2,1)} %constant.17.clone.col_low_any) | copy-start | bytes 1572868
  3.9 1.0 %copy-start.2 = (bf16[512,512]{1,0:T(8,128)(2,1)S(1)}, bf16[512,512]{1,0:T(8,128)(2,1)}, u32[]{:S(2)}) copy-start(bf16[512,512]{1,0:T(8,128)(2,1)} %constant.16.clone.col_high_any) | copy-start | bytes 1572868
  4.9 0.8 %copy-start.3 = (bf16[1,3,2,8,512]{4,3,2,1,0:T(8,128)(2,1)S(1)}, bf16[1,3,2,8,512]{4,3,2,1,0:T(8,128)(2,1)}, u32[]{:S(2)}) copy-start(bf16[1,3,2,8,512]{4,3,2,1,0:T(8,128)(2,1)} %target.1) | copy-start | bytes 147460
  5.7 0.7 %copy-start.4 = (bf16[3,3,3,3,128]{4,3,2,1,0:T(4,128)(2,1)S(1)}, bf16[3,3,3,3,128]{4,3,2,1,0:T(4,128)(2,1)}, u32[]{:S(2)}) copy-start(bf16[3,3,3,3,128]{4,3,2,1,0:T(4,128)(2,1)} %weight.1) | copy-start | bytes 62212
  6.4 0.7 %copy-start.5 = (bf16[64,64]{1,0:T(8,128)(2,1)S(1)}, bf16[64,64]{1,0:T(8,128)(2,1)}, u32[]{:S(2)}) copy-start(bf16[64,64]{1,0:T(8,128)(2,1)} %constant.15.clone.back_low) | copy-start | bytes 24580
  7.2 0.7 %copy-start.6 = (bf16[64,64]{1,0:T(8,128)(2,1)S(1)}, bf16[64,64]{1,0:T(8,128)(2,1)}, u32[]{:S(2)}) copy-start(bf16[64,64]{1,0:T(8,128)(2,1)} %constant.14.clone.back_high) | copy-start | bytes 24580
  7.9 0.7 %copy-start.7 = (bf16[64,64]{1,0:T(8,128)(2,1)S(1)}, bf16[64,64]{1,0:T(8,128)(2,1)}, u32[]{:S(2)}) copy-start(bf16[64,64]{1,0:T(8,128)(2,1)} %constant.13.clone.row_low) | copy-start | bytes 24580
  8.6 0.7 %copy-start.8 = (bf16[64,64]{1,0:T(8,128)(2,1)S(1)}, bf16[64,64]{1,0:T(8,128)(2,1)}, u32[]{:S(2)}) copy-start(bf16[64,64]{1,0:T(8,128)(2,1)} %constant.12.clone.row_high) | copy-start | bytes 24580

commit v2 on v1

--- a/solution.py
+++ b/solution.py
@@ -67,19 +67,16 @@
     features,
     weight,
     target,
-    row_high,
-    row_low,
-    back_high,
-    back_low,
-    col_high_any,
-    col_low_any,
-    shifted_out,
-    weight_out,
+    row_tables,
+    col_tables,
+    grad_features,
     grad_weight,
     loss_out,
     held,
-    col_high,
-    col_low,
+    weight_in,
+    target_in,
+    row_held,
+    col_held,
     acc,
     weight_acc,
     part,
@@ -116,9 +113,10 @@
         pltpu.make_async_copy(features.at[0, f], held.at[f], load_sem.at[f])
         for f in range(frames_in)
     ]
-    loads.append(pltpu.make_async_copy(col_high_any, col_high, load_sem.at[frames_in]))
-    loads.append(pltpu.make_async_copy(col_low_any, col_low, load_sem.at[frames_in + 1]))
-    for load in loads:
+    small = ((weight, weight_in), (target, target_in), (row_tables, row_held), (col_tables, col_held))
+    for at, (source, place) in enumerate(small):
+        loads.append(pltpu.make_async_copy(source, place, load_sem.at[frames_in + at]))
+    for load in loads[frames_in : frames_in + 2] + loads[:frames_in] + loads[frames_in + 2 :]:
         load.start()
 
     barrier = pltpu.get_barrier_semaphore()
@@ -144,21 +142,21 @@
         )
 
     weight_acc[...] = jnp.zeros_like(weight_acc)
+    acc[...] = jnp.zeros_like(acc)
+    loads[frames_in].wait()
+    loads[frames_in + 1].wait()
     for dt in range(3):
         for di in range(3):
             for dj in range(3):
                 at = (dt * 3 + di) * BLOCK + dj * 3
-                weight_acc[at : at + 3, :] = weight[dt, di, dj].astype(F32)
+                weight_acc[at : at + 3, :] = weight_in[dt, di, dj].astype(F32)
     taps = weight_acc[...].astype(BF16)
-    weight_out[...] = taps
-
-    acc[...] = jnp.zeros_like(acc)
 
     @pl.when(ch == 0)
     def _():
         for t in range(frames_out):
             for o in range(3):
-                frame = -target[0, o, t].astype(F32)
+                frame = -target_in[0, o, t].astype(F32)
                 for i in range(rows_dev):
                     acc[t, rows_dev - i, 3 + o, :] = frame[i]
 
@@ -200,8 +198,8 @@
         if f >= 2:
             exchange(f - 2)
 
-    loads[frames_in].wait()
-    loads[frames_in + 1].wait()
+    loads[frames_in + 2].wait()
+    loads[frames_in + 3].wait()
 
     @pl.when(me < planes)
     def _():
@@ -222,8 +220,8 @@
         residual = jnp.concatenate(blocks, axis=0)
         height = n_row * rows_dev
         half = columns // 2
-        basis = (col_high[...], col_low[...])
-        rows_done = dot3((row_high[...], row_low[...]), halves(residual))
+        basis = (col_held[0], col_held[1])
+        rows_done = dot3((row_held[0], row_held[1]), halves(residual))
         both = dot3(halves(rows_done), basis)
         real = both[:height, :half] - both[height:, half:]
         imag = both[height:, :half] + both[:height, half:]
@@ -241,7 +239,7 @@
             axis=0,
         )
         columns_done = dot3(halves(upstream), basis, ((1,), (1,)))
-        grads = dot3((back_high[...], back_low[...]), halves(columns_done))
+        grads = dot3((row_held[2], row_held[3]), halves(columns_done))
         loss_high = loss.astype(BF16).astype(F32)
         loss_mid = (loss - loss_high).astype(BF16).astype(F32)
         loss_low = loss - loss_high - loss_mid
@@ -290,7 +288,6 @@
     loss_out[...] = loss_total
     for t in range(frames_out):
         shifted[t] = acc[t].reshape(BLOCK * BLOCK, columns).astype(BF16)
-    shifted_out[...] = shifted[...]
 
     kernel_acc[...] = jnp.zeros_like(kernel_acc)
 
@@ -326,6 +323,20 @@
                 device_id_type=MESH,
             ).start()
 
+    def pull(f):
+        low, top = max(0, f - frames_out + 1), min(2, f)
+        chosen = taps[low * 3 * BLOCK : (top + 1) * 3 * BLOCK]
+        for r in range(rows_dev):
+            begin = (rows_dev - 1 - r) * BLOCK
+            stack = jnp.concatenate(
+                [shifted[f - dt, begin : begin + 3 * BLOCK, :] for dt in range(low, top + 1)],
+                axis=0,
+            )
+            grad_features[0, f, r] = dot(stack, chosen, ((0,), (0,))).astype(BF16)
+
+    for f in range(frames_in // 2):
+        pull(f)
+
     @pl.when(rank < n_own)
     def _():
         @pl.loop(0, n_all)
@@ -350,6 +361,9 @@
                 device_id_type=MESH,
             ).start()
 
+    for f in range(frames_in // 2, frames_in):
+        pull(f)
+
     for m in range(n_own):
         @pl.when(rank != m)
         def _():
@@ -387,22 +401,6 @@
             pltpu.make_async_copy(
                 terms_sum.at[rank], terms_sum.at[rank], sum_send.at[p]
             ).wait()
-
-
-def features_kernel(frames_out, shifted, taps, grad):
-    rows_dev, columns, channels = grad.shape[2:]
-    for f in range(frames_out + 2):
-        @pl.when(pl.program_id(0) == f)
-        def _():
-            low, top = max(0, f - frames_out + 1), min(2, f)
-            chosen = taps[low * 3 * BLOCK : (top + 1) * 3 * BLOCK, :]
-            for r in range(rows_dev):
-                begin = (rows_dev - 1 - r) * BLOCK
-                stack = jnp.concatenate(
-                    [shifted[f - dt, begin : begin + 3 * BLOCK, :] for dt in range(low, top + 1)],
-                    axis=0,
-                )
-                grad[0, 0, r] = dot(stack, chosen, ((0,), (0,))).astype(BF16)
 
 
 def shards(features, weight, target):
@@ -417,28 +415,31 @@
     chunk = 8 * -(-pieces // n_all)
     n_own = -(-81 // chunk)
     rows = row_table(height, rows_dev)
-    tables = (
-        *split_table(rows),
-        *split_table(np.ascontiguousarray(rows.T)),
-        *split_table(column_table(columns)),
+    assert BLOCK == 2 * rows_dev
+    row_tables = np.stack(split_table(rows) + split_table(rows.T))
+    col_tables = np.stack(split_table(column_table(columns)))
+    vmem = pl.BlockSpec(memory_space=pltpu.VMEM)
+    inputs = tuple(
+        pltpu.with_memory_space_constraint(x, pltpu.HBM)
+        for x in (features, weight, target, jnp.asarray(row_tables), jnp.asarray(col_tables))
     )
-    vmem = pl.BlockSpec(memory_space=pltpu.VMEM)
-    anywhere = pl.BlockSpec(memory_space=pl.ANY)
+    hbm = pl.BlockSpec(memory_space=pltpu.HBM)
     dma = pltpu.SemaphoreType.DMA
-    shifted, taps, grad_weight, loss = pl.pallas_call(
+    grad_features, grad_weight, loss = pl.pallas_call(
         functools.partial(main_kernel, (n_clip, n_row, n_ch, chunk, n_own)),
         out_shape=(
-            jax.ShapeDtypeStruct((frames_out, BLOCK * BLOCK, columns), BF16),
-            jax.ShapeDtypeStruct((9 * BLOCK, channels), BF16),
+            jax.ShapeDtypeStruct(features.shape, BF16),
             jax.ShapeDtypeStruct((3, 3, 3, 3, channels), F32),
             jax.ShapeDtypeStruct((1, 128), F32),
         ),
-        in_specs=[anywhere] + [vmem] * 6 + [anywhere] * 2,
-        out_specs=(vmem,) * 4,
+        in_specs=[hbm] * 5,
+        out_specs=(vmem,) * 3,
         scratch_shapes=[
             pltpu.VMEM((frames_in, rows_dev, columns, channels), BF16),
-            pltpu.VMEM((columns, columns), BF16),
-            pltpu.VMEM((columns, columns), BF16),
+            pltpu.VMEM(weight.shape, BF16),
+            pltpu.VMEM(target.shape, BF16),
+            pltpu.VMEM(row_tables.shape, BF16),
+            pltpu.VMEM(col_tables.shape, BF16),
             pltpu.VMEM((frames_out, BLOCK, BLOCK, columns), F32),
             pltpu.VMEM((9 * BLOCK, channels), F32),
             pltpu.VMEM((planes, BLOCK, columns), F32),
@@ -450,7 +451,7 @@
             pltpu.VMEM((n_own * chunk, channels), F32),
             pltpu.VMEM((n_all, chunk, channels), F32),
             pltpu.VMEM((n_own, chunk, channels), F32),
-            dma((frames_in + 2,)),
+            dma((frames_in + 4,)),
             dma((planes,)),
             dma((n_group,)),
             dma((n_group,)),
@@ -464,21 +465,7 @@
             collective_id=0, has_side_effects=True, vmem_limit_bytes=48 * 1024 * 1024
         ),
         name="main",
-    )(features, weight, target, *tables)
-    grad_features = pl.pallas_call(
-        functools.partial(features_kernel, frames_out),
-        grid=(frames_in,),
-        out_shape=jax.ShapeDtypeStruct(features.shape, BF16),
-        in_specs=[
-            pl.BlockSpec(shifted.shape, lambda f: (0, 0, 0)),
-            pl.BlockSpec(taps.shape, lambda f: (0, 0)),
-        ],
-        out_specs=pl.BlockSpec(
-            (1, 1, rows_dev, columns, channels), lambda f: (0, f, 0, 0, 0)
-        ),
-        compiler_params=pltpu.CompilerParams(vmem_limit_bytes=48 * 1024 * 1024),
-        name="features",
-    )(shifted, taps)
+    )(*inputs)
     return (grad_features, grad_weight, loss[0, :1])
 
 

time: 41.5 us -> 30.6 us (0.74); the launches traced: 40.9 us -> 30.4 us
  local copies, waits for them, and re-layouts: 9.29 us -> 2.64 us
  Pallas kernels: 29.8 us -> 26 us
    unnamed x19 -> x2, local copies, waits for them, and re-layouts: 9.29 us -> 2.64 us
    pallas_call x1 -> x0, Pallas kernels: 3.43 us -> none  [shards(): pl.pallas_call(functools.partial(features_kernel, frames_out), grid=(fram...]
where the time goes in v2:
time: 30.6 us; the launch traced here: 30.4 us
  Pallas kernels  26 us (85%)
  local copies, waits for them, and re-layouts  2.64 us (9%)
  between operations  1.8 us (6%)
    pallas_call x1, Pallas kernels, shards(): pl.pallas_call(functools.partial(main_kernel, (n_clip, n_row, n_ch, chunk...  26 us
    unnamed x2, local copies, waits for them, and re-layouts  2.64 us

profile of v2, /device:TPU:0, one launch (start us, length us, event | category | flops | bytes accessed | tf_op | source)
XLA Modules:
  0.0 30.4 jit_solution(14000545637460621251)
XLA Ops:
  0.6 26.0 %main.1 = (bf16[1,4,8,512,128]{4,3,2,1,0:T(8,128)(2,1)S(1)}, f32[3,3,3,3,128]{4,3,2,1,0:T(4,128)S(1)}, f32[1,128]{1,0:T(1,128)S(1)}) custom-call(bf16[1,4,8,512,128]{4,3,2,1,0:T(8,128)(2,1)} %features.1, bf16[3,3,3,3,128]{4,3,2,1,0:T(4,128)(2,1)} %weight.1, bf16[1,3,2,8,512]{4,3,2,1,0:T(8,128)(2,1)} %target.1, bf16[4,64,64]{2,1,0:T(8,128)(2,1)} %constant.4.clone.row_tables, ...), custom_call_target="tpu_custom_call" | custom-call | tf_op jit(solution)/shard_map/main/pallas_call | solution.py:428
  26.6 2.0 %copy.11 = bf16[1,4,8,512,128]{4,3,2,1,0:T(8,128)(2,1)} copy(bf16[1,4,8,512,128]{4,3,2,1,0:T(8,128)(2,1)S(1)} %get-tuple-element.12) | data formatting | bytes 8388608
  28.6 0.6 %copy.12 = f32[3,3,3,3,128]{4,3,2,1,0:T(4,128)} copy(f32[3,3,3,3,128]{4,3,2,1,0:T(4,128)S(1)} %get-tuple-element.13) | data formatting | bytes 82944

commit v3 on v2

--- a/solution.py
+++ b/solution.py
@@ -51,7 +51,23 @@
 
 
 def dot3(a, b, dims=((1,), (0,))):
-    return dot(a[0], b[0], dims) + (dot(a[0], b[1], dims) + dot(a[1], b[0], dims))
+    count = a[0].shape[0]
+    both = dot(jnp.concatenate(a, axis=0), b[0], dims)
+    return both[:count] + (both[count:] + dot(a[0], b[1], dims))
+
+
+def swap_table(rows, columns):
+    left = lax.broadcasted_iota(jnp.int32, (rows, columns), 0)
+    right = lax.broadcasted_iota(jnp.int32, (rows, columns), 1)
+    match = (left // BLOCK == right % BLOCK) & (left % BLOCK == right // BLOCK)
+    return match.astype(F32).astype(BF16)
+
+
+def plane_owners(planes, n_row, n_ch):
+    if planes == 6 and n_row % 4 == 0 and n_ch == 2:
+        places = ((0, 0), (3, 1), (0, 1), (1, 0), (2, 1), (2, 0))
+        return [(row * (n_row // 4), ch) for row, ch in places]
+    return [(plane // n_ch, plane % n_ch) for plane in range(planes)]
 
 
 def shift(x, by):
@@ -106,6 +122,12 @@
     n_all = n_clip * n_row
     clip, row, ch = (lax.axis_index(a) for a in ("clip", "row", "ch"))
     me = row * n_ch + ch
+    owners = plane_owners(planes, n_row, n_ch)
+    slots = [at_row * n_ch + at_ch for at_row, at_ch in owners]
+    owning = me == slots[0]
+    for slot in slots[1:]:
+        owning = owning | (me == slot)
+    lines = (rows_dev + 2) * BLOCK
     rank = clip * n_row + row
     entries = float(planes * n_row * rows_dev * (columns // 2))
 
@@ -158,26 +180,36 @@
             for o in range(3):
                 frame = -target_in[0, o, t].astype(F32)
                 for i in range(rows_dev):
-                    acc[t, rows_dev - i, 3 + o, :] = frame[i]
+                    acc[t, (rows_dev - i) * BLOCK + 3 + o, :] = frame[i]
+
+    swap = swap_table(9 * BLOCK, lines)
+    swap_back = swap_table(lines, 9 * BLOCK)
 
     def exchange(t):
+        high, low = halves(acc[t])
+        swapped = dot(swap, high) + dot(swap, low)
+        third = 3 * BLOCK
+        frame = (
+            swapped[third : 2 * third]
+            + shift(swapped[:third], 1)
+            + shift(swapped[2 * third :], -1)
+        )
         for o in range(3):
-            views = [acc[t, :, dj * 3 + o, :] for dj in range(3)]
-            part[t * 3 + o] = views[1] + shift(views[0], 1) + shift(views[2], -1)
             plane = t * 3 + o
-
-            @pl.when(me == plane)
+            part[plane] = frame[o * BLOCK : (o + 1) * BLOCK]
+
+            @pl.when(me == slots[plane])
             def _():
-                arrived[plane] = part[plane]
-
-            @pl.when(me != plane)
+                arrived[slots[plane]] = part[plane]
+
+            @pl.when(me != slots[plane])
             def _():
                 pltpu.make_async_remote_copy(
                     src_ref=part.at[plane],
                     dst_ref=arrived.at[me],
                     send_sem=send_sem.at[plane],
                     recv_sem=recv_sem.at[me],
-                    device_id={"row": plane // n_ch, "ch": plane % n_ch},
+                    device_id={"row": owners[plane][0], "ch": owners[plane][1]},
                     device_id_type=MESH,
                 ).start()
 
@@ -188,10 +220,11 @@
 
         @pl.loop(0, rows_dev, unroll=True)
         def _(r):
-            made = dot(chosen, held[f, r], ((1,), (1,))).reshape(-1, BLOCK, columns)
+            made = dot(chosen, held[f, r], ((1,), (1,)))
+            begin = pl.multiple_of((rows_dev - 1 - r) * BLOCK, BLOCK)
             for dt in range(low, top + 1):
-                at = (dt - low) * 3
-                acc[f - dt, pl.ds(rows_dev - 1 - r, 3)] += made[at : at + 3]
+                at = (dt - low) * 3 * BLOCK
+                acc[f - dt, pl.ds(begin, 3 * BLOCK), :] += made[at : at + 3 * BLOCK]
 
         if f == 2:
             pl.semaphore_wait(barrier, n_group - 1 + n_all - n_row)
@@ -201,15 +234,14 @@
     loads[frames_in + 2].wait()
     loads[frames_in + 3].wait()
 
-    @pl.when(me < planes)
+    @pl.when(owning)
     def _():
         @pl.loop(0, n_group)
         def _(s):
             @pl.when(s != me)
             def _():
-                pltpu.make_async_copy(
-                    arrived.at[s], arrived.at[s], recv_sem.at[s]
-                ).wait()
+                piece = arrived.at[s]
+                pltpu.make_async_copy(piece, piece, recv_sem.at[s]).wait()
 
         blocks = []
         for r in range(n_row):
@@ -265,29 +297,23 @@
 
         grad_all[me] = grad_send[row]
 
-    acc[...] = jnp.zeros_like(acc)
-    for plane in range(planes):
-        @pl.when(me != plane)
-        def _():
-            pltpu.make_async_copy(
-                grad_all.at[plane], grad_all.at[plane], back_recv.at[plane]
-            ).wait()
-
     loss_total = jnp.zeros((1, 128), F32)
-    for plane in range(planes):
-        t, o = divmod(plane, 3)
-        grads = grad_all[plane].astype(F32)
-        for part_at in range(3):
-            at = rows_dev + 2 + part_at
-            loss_total = loss_total + grads[at : at + 1, :128]
-        entry = lax.broadcasted_iota(jnp.int32, grads.shape, 0)
-        grads = jnp.where(entry < rows_dev + 2, grads, 0.0)
-        for dj in range(3):
-            moved = grads if dj == 1 else shift(grads, dj - 1)
-            acc[t, :, dj * 3 + o, :] = moved
+    for t in range(frames_out):
+        for slot in slots[3 * t : 3 * t + 3]:
+            @pl.when(me != slot)
+            def _():
+                pltpu.make_async_copy(
+                    grad_all.at[slot], grad_all.at[slot], back_recv.at[slot]
+                ).wait()
+
+        frame = jnp.concatenate([grad_all[slot] for slot in slots[3 * t : 3 * t + 3]], axis=0)
+        frame = frame.astype(F32)
+        for o in range(3):
+            for at in range(rows_dev + 2, rows_dev + 5):
+                loss_total = loss_total + frame[o * BLOCK + at : o * BLOCK + at + 1, :128]
+        moved = jnp.concatenate([shift(frame, -1), frame, shift(frame, 1)], axis=0)
+        shifted[t] = dot(swap_back, moved.astype(BF16)).astype(BF16)
     loss_out[...] = loss_total
-    for t in range(frames_out):
-        shifted[t] = acc[t].reshape(BLOCK * BLOCK, columns).astype(BF16)
 
     kernel_acc[...] = jnp.zeros_like(kernel_acc)
 
@@ -378,11 +404,12 @@
             grad_weight[dt, di, dj, o : o + 1, :] = terms_sum[m, at : at + 1, :]
 
     for plane in range(planes):
-        @pl.when(me != plane)
+        @pl.when(me != slots[plane])
         def _():
-            pltpu.make_async_copy(part.at[plane], part.at[plane], send_sem.at[plane]).wait()
-
-    @pl.when(me < planes)
+            piece = part.at[plane]
+            pltpu.make_async_copy(piece, piece, send_sem.at[plane]).wait()
+
+    @pl.when(owning)
     def _():
         @pl.loop(1, n_group)
         def _(p):
@@ -440,13 +467,13 @@
             pltpu.VMEM(target.shape, BF16),
             pltpu.VMEM(row_tables.shape, BF16),
             pltpu.VMEM(col_tables.shape, BF16),
-            pltpu.VMEM((frames_out, BLOCK, BLOCK, columns), F32),
+            pltpu.VMEM((frames_out, (rows_dev + 2) * BLOCK, columns), F32),
             pltpu.VMEM((9 * BLOCK, channels), F32),
             pltpu.VMEM((planes, BLOCK, columns), F32),
             pltpu.VMEM((n_group, BLOCK, columns), F32),
             pltpu.VMEM((n_row, BLOCK, columns), BF16),
-            pltpu.VMEM((planes, BLOCK, columns), BF16),
-            pltpu.VMEM((frames_out, BLOCK * BLOCK, columns), BF16),
+            pltpu.VMEM((n_group, BLOCK, columns), BF16),
+            pltpu.VMEM((frames_out, (rows_dev + 2) * BLOCK, columns), BF16),
             pltpu.VMEM((9 * BLOCK, channels), F32),
             pltpu.VMEM((n_own * chunk, channels), F32),
             pltpu.VMEM((n_all, chunk, channels), F32),
@@ -455,7 +482,7 @@
             dma((planes,)),
             dma((n_group,)),
             dma((n_group,)),
-            dma((planes,)),
+            dma((n_group,)),
             dma((n_own,)),
             dma((n_all,)),
             dma((n_all,)),

time: 30.6 us -> 30.7 us (level)
  no operation moved by 1% of the time
where the time goes in v3:
time: 30.7 us; the launch traced here: 30.5 us
  Pallas kernels  26.1 us (85%)
  local copies, waits for them, and re-layouts  2.64 us (9%)
  between operations  1.8 us (6%)
    pallas_call x1, Pallas kernels, shards(): pl.pallas_call(functools.partial(main_kernel, (n_clip, n_row, n_ch, chunk...  26.1 us
    unnamed x2, local copies, waits for them, and re-layouts  2.64 us

profile of v3, /device:TPU:0, one launch (start us, length us, event | category | flops | bytes accessed | tf_op | source)
XLA Modules:
  0.0 30.5 jit_solution(8687325613941231484)
XLA Ops:
  0.6 26.1 %main.1 = (bf16[1,4,8,512,128]{4,3,2,1,0:T(8,128)(2,1)S(1)}, f32[3,3,3,3,128]{4,3,2,1,0:T(4,128)S(1)}, f32[1,128]{1,0:T(1,128)S(1)}) custom-call(bf16[1,4,8,512,128]{4,3,2,1,0:T(8,128)(2,1)} %features.1, bf16[3,3,3,3,128]{4,3,2,1,0:T(4,128)(2,1)} %weight.1, bf16[1,3,2,8,512]{4,3,2,1,0:T(8,128)(2,1)} %target.1, bf16[4,64,64]{2,1,0:T(8,128)(2,1)} %constant.4.clone.row_tables, ...), custom_call_target="tpu_custom_call" | custom-call | tf_op jit(solution)/shard_map/main/pallas_call | solution.py:455
  26.7 2.0 %copy.11 = bf16[1,4,8,512,128]{4,3,2,1,0:T(8,128)(2,1)} copy(bf16[1,4,8,512,128]{4,3,2,1,0:T(8,128)(2,1)S(1)} %get-tuple-element.12) | data formatting | bytes 8388608
  28.8 0.6 %copy.12 = f32[3,3,3,3,128]{4,3,2,1,0:T(4,128)} copy(f32[3,3,3,3,128]{4,3,2,1,0:T(4,128)S(1)} %get-tuple-element.13) | data formatting | bytes 82944
